TPU v7x, 512 devices: a whole 4x8x8 slice. The times are simulated.
512 devices in a mesh: row: 32 (over y_hi, z), col: 16 (over x, y_lo, core).
Axes of the slice: x: 4, y: 8 (y_hi: 4, y_lo: 2; y = y_hi * 2 + y_lo), z: 8, core: 2. Of those that a mesh axis runs over, the one named last changes fastest.
Arguments:
- positions: float32 [3, 262144], P(None, ('row', 'col')), as said below
- velocities: float32 [3, 262144], P(None, ('row', 'col')), may hold values from -2.5 to 2.5
- bead_types: int32 [262144], P(('row', 'col')), may hold values from 0 to 17
- slot_bead: int32 [262144], P(('row', 'col')), may hold values from 0 to 511, as said below
- tile_pairs: int32 [2, 36864], P(None, ('row', 'col')), may hold values from 0 to 127, as said below
- tile_count: int32 [512], P(('row', 'col')), may hold values from 1 to 72, as said below
- c6_table: float32 [18, 18], replicated, as said below
- c12_table: float32 [18, 18], replicated, as said below
Outputs:
- kicked: float32 [3, 262144], P(None, ('row', 'col'))
Inputs may be any that keep to these rules, and one draw needn't show every extreme that they name: `positions`: the beads of block k of device d = r * 16 + c lie in the cell [u, u + 1) x [v, v + 1) x [k, k + 1), in units of 2.47 nm, with u = 2 (c % 8) + c // 8 and v = 2 (r % 16) + r // 16: a slab periodic in its first two dimensions. `slot_bead`: each device's values are a permutation of 0 to 511. `tile_pairs`: the first row is below 64, the second below 128; the 72 (i-block, j-block) pairs of a device are distinct, and the cells of the two blocks are equal or touch, counting periodic images in the first two dimensions. `tile_count`: A device's live tiles are its first slots. Of the two devices of a row whose col indices differ only in the lowest bit, one has 72 live tiles and the other at most 24; some pair reaches 24 in every draw. `c6_table`: Symmetric. `c12_table`: Symmetric.
All inputs are finite; a program needn't handle non-finite values.
Results may differ from a plain program's by a relative error of at most 0.0003.
Values sent between devices are 32-bit elements; how exact they have to be, the bound alone decides.
A program may use at most 64 MiB of HBM per device.

v0:
```python
import math

import jax
import jax.numpy as jnp
from jax import lax
from jax.sharding import PartitionSpec as P

SOFT_CORE = 0.25
CUT_OFF = 1.2
CELL_SIDE = 2.47
KICK_FACTOR = 0.02 / 72.0
HIGH = lax.Precision.HIGHEST


def pair_forces(i_beads, j_beads, i_table6, i_table12, j_onehot, live, j_keep, box_x, box_y):
    offset = i_beads[:, :, :, None] - j_beads[:, :, None, :]
    off_x = offset[0] - box_x * jnp.floor(offset[0] / box_x + 0.5)
    off_y = offset[1] - box_y * jnp.floor(offset[1] / box_y + 0.5)
    off_z = offset[2]
    dist_sq = off_x * off_x + off_y * off_y + off_z * off_z
    coef6 = jnp.einsum("kba,kbc->bac", i_table6, j_onehot, precision=HIGH)
    coef12 = jnp.einsum("kba,kbc->bac", i_table12, j_onehot, precision=HIGH)
    inverse = 1.0 / (dist_sq + SOFT_CORE)
    inverse3 = inverse * inverse * inverse
    cut_inv = 1.0 / (CUT_OFF * CUT_OFF + SOFT_CORE)
    cut3 = cut_inv * cut_inv * cut_inv
    scalar = (12.0 * coef12 * inverse3 * inverse3 - 6.0 * coef6 * inverse3) * inverse
    scalar = scalar - (12.0 * coef12 * cut3 * cut3 - 6.0 * coef6 * cut3) * cut_inv
    scalar = jnp.where(dist_sq < CUT_OFF * CUT_OFF, scalar, 0.0) * live[:, None, None]
    weighted = scalar[None] * jnp.stack([off_x, off_y, off_z])
    return (jnp.sum(weighted, axis=3), -jnp.sum(weighted, axis=2) * j_keep[:, None])


def run_tiles(
    i_xyz, i_tab6, i_tab12, j_xyz, j_onehot, i_block, j_block, live, j_keep, box_x, box_y
):
    total = i_block.shape[0]
    size = math.gcd(total, 8)
    items = tuple((a.reshape(total // size, size) for a in (i_block, j_block, live, j_keep)))
    init = (jnp.zeros(i_xyz.shape, jnp.float32), jnp.zeros(j_xyz.shape, jnp.float32))

    def step(carry, item):
        i_sel, j_sel, alive, keep = item
        force_i, force_j = pair_forces(
            jnp.take(i_xyz, i_sel, axis=1),
            jnp.take(j_xyz, j_sel, axis=1),
            jnp.take(i_tab6, i_sel, axis=1),
            jnp.take(i_tab12, i_sel, axis=1),
            jnp.take(j_onehot, j_sel, axis=1),
            alive,
            keep,
            box_x,
            box_y,
        )
        return ((carry[0].at[:, i_sel].add(force_i), carry[1].at[:, j_sel].add(force_j)), None)

    result, _ = lax.scan(step, init, items)
    return result


def type_onehot(kinds, ntypes):
    return (kinds[None, :] == jnp.arange(ntypes, dtype=jnp.float32)[:, None]).astype(jnp.float32)


def global_j(local_j, j_col, per_dev, cols):
    return (local_j // per_dev * cols + j_col) * per_dev + local_j % per_dev


def body(positions, velocities, bead_types, slot_bead, tile_pairs, tile_count, c6_table, c12_table):
    group = positions.shape[1]
    per_dev = group // 128
    slots = tile_pairs.shape[1]
    ntypes = c6_table.shape[0]
    rows = lax.axis_size("row")
    cols = lax.axis_size("col")
    box_x = cols * CELL_SIDE
    box_y = rows * CELL_SIDE
    row_at = lax.axis_index("row")
    col_at = lax.axis_index("col")
    ordered = jnp.take(positions, slot_bead, axis=1)
    kinds = jnp.take(bead_types, slot_bead).astype(jnp.float32)
    packed = jnp.concatenate([ordered, kinds[None, :]], axis=0)
    i_all = lax.all_gather(packed, "col", axis=1, tiled=True)
    i_onehot = type_onehot(i_all[3], ntypes)
    i_tab6 = jnp.dot(c6_table, i_onehot, precision=HIGH).reshape(ntypes, -1, 128)
    i_tab12 = jnp.dot(c12_table, i_onehot, precision=HIGH).reshape(ntypes, -1, 128)
    i_xyz = i_all[:3].reshape(3, -1, 128)
    i_first = row_at * cols * per_dev
    j_all = lax.all_gather(packed, "row", axis=1, tiled=True)
    j_xyz = j_all[:3].reshape(3, -1, 128)
    j_onehot = type_onehot(j_all[3], ntypes).reshape(ntypes, -1, 128)
    i_block = tile_pairs[0]
    j_block = tile_pairs[1]
    alive = jnp.arange(slots, dtype=jnp.int32) < tile_count[0]
    same = i_first + i_block == global_j(j_block, col_at, per_dev, cols)
    live = alive.astype(jnp.float32)
    j_keep = (alive & jnp.logical_not(same)).astype(jnp.float32)
    i_part, j_part = run_tiles(
        i_xyz, i_tab6, i_tab12, j_xyz, j_onehot, i_block, j_block, live, j_keep, box_x, box_y
    )
    j_force = lax.psum_scatter(j_part.reshape(3, -1), "row", scatter_dimension=1, tiled=True)
    i_force = lax.psum_scatter(i_part.reshape(3, -1), "col", scatter_dimension=1, tiled=True)
    total = i_force + j_force
    return velocities.at[:, slot_bead].add(KICK_FACTOR * total)


def solution(mesh):
    return jax.shard_map(
        body,
        mesh=mesh,
        in_specs=(
            P(None, ("row", "col")),
            P(None, ("row", "col")),
            P(("row", "col")),
            P(("row", "col")),
            P(None, ("row", "col")),
            P(("row", "col")),
            P(),
            P(),
        ),
        out_specs=P(None, ("row", "col")),
        check_vma=False,
    )
```

profile of v0, /device:TPU:1, one launch (start us, length us, event | category | flops | bytes accessed | tf_op | source)
XLA Modules:
  0.0 552.9 jit_solution(7952668310688254442)
XLA Ops:
  7.3 3.6 gather_fusion.6
  12.4 23.2 %all_gather.6 = f32[4,8192]{1,0:T(4,128)S(1)} all-gather(f32[4,512]{1,0:T(4,128)S(1)} %pad_maximum_fusion), channel_id=1, replica_groups=mesh['row'=32,'col'=16] {'col'}, dimensions={1}, use_global_device_ids=true | all-gather | bytes 139264 | tf_op jit(solution)/shard_map/all_gather | solution.py:83
  35.6 72.8 %all_gather.7 = f32[4,16384]{1,0:T(4,128)S(1)} all-gather(f32[4,512]{1,0:T(4,128)S(1)} %pad_maximum_fusion), channel_id=1, replica_groups=mesh['row'=32,'col'=16] {'row'}, dimensions={1}, use_global_device_ids=true | all-gather | bytes 270336 | tf_op jit(solution)/shard_map/all_gather | solution.py:89
  110.6 1.2 copy.36
  113.3 103.9 %while.17 = (s32[]{:T(128)}, f32[3,64,128]{2,0,1:T(4,128)S(1)}, f32[3,128,128]{2,0,1:T(4,128)S(1)}, s32[9,8]{1,0:T(8,128)S(1)}, f32[3,64,128]{2,0,1:T(4,128)S(1)...) while((s32[]{:T(128)}, f32[3,64,128]{2,0,1:T(4,128)S(1)}, ...), condition=%wide.region_5.7_spmd.clone, body=%wide.region_0.6_spmd.clone.sunk | while | flops 65428624 | bytes 14666097 | solution.py:57
  117.8 1.7 gather_fusion.4
  120.2 2.2 fusion.74
  126.3 1.1 fusion.72
  129.3 1.7 gather_fusion.4
  131.7 2.2 fusion.74
  137.9 1.1 fusion.72
  140.9 1.7 gather_fusion.4
  143.3 2.2 fusion.74
  152.4 1.7 gather_fusion.4
  154.8 2.2 fusion.74
  161.0 1.1 fusion.72
  163.9 1.7 gather_fusion.4
  166.3 2.2 fusion.74
  175.5 1.7 gather_fusion.4
  177.9 2.2 fusion.74
  187.0 1.7 gather_fusion.4
  189.4 2.2 fusion.74
  198.6 1.7 gather_fusion.4
  201.0 2.2 fusion.74
  207.1 1.1 fusion.72
  210.1 1.7 gather_fusion.4
  212.5 2.2 fusion.74
  217.2 2.7 copy.40
  220.0 5.1 copy.42
  225.9 71.0 %reduce-scatter.7.cloned.1.call-done = f32[512,3]{1,0:T(8,128)} async-done(((f32[8192,3]{1,0:T(8,128)}), f32[512,3]{1,0:T(8,128)}) %reduce-scatter.7.cloned.1.call-update) | async-done | bytes 6160
  298.0 242.6 %reduce-scatter.9.cloned.1.call-done = f32[512,3]{1,0:T(8,128)} async-done(((f32[16384,3]{1,0:T(8,128)}), f32[512,3]{1,0:T(8,128)}) %reduce-scatter.9.cloned.1.call-update) | async-done | bytes 6160
  541.8 3.6 scatter_fusion.2
  (515 shorter events, 70.4 us)
Async XLA Ops:
  6.5 102.0 %copy-start = (f32[18,18]{1,0:T(8,128)S(1)}, f32[18,18]{1,0:T(8,128)}, u32[]{:S(2)}) copy-start(f32[18,18]{1,0:T(8,128)} %param.19) | copy-start | bytes 3892
  6.5 4.4 copy-start.20
  6.5 4.4 copy-start.18
  6.5 290.4 %reduce-scatter.7.cloned.1.call-start = ((), (), s32[]{:S(2)}) async-start(), calls=%async_computation.2 | async-start | bytes 4456448
  113.4 4.3 copy-start.11
  113.4 4.3 copy-start.13
  124.9 3.9 copy-start.1
  124.9 3.9 copy-start.3
  124.9 4.4 copy-start.11
  124.9 4.4 copy-start.13
  136.4 3.9 copy-start.1
  136.5 3.9 copy-start.3
  136.5 4.4 copy-start.11
  136.5 4.4 copy-start.13
  148.0 4.3 copy-start.11
  148.0 4.3 copy-start.13
  159.5 3.9 copy-start.1
  159.5 3.9 copy-start.3
  159.5 4.4 copy-start.11
  159.6 4.4 copy-start.13
  171.1 3.9 copy-start.1
  171.1 3.9 copy-start.3
  171.1 4.4 copy-start.11
  171.1 4.4 copy-start.13
  182.6 4.3 copy-start.11
  182.6 4.3 copy-start.13
  194.2 4.4 copy-start.11
  194.2 4.4 copy-start.13
  205.7 4.4 copy-start.11
  205.7 4.4 copy-start.13
  219.9 320.6 %reduce-scatter.9.cloned.1.call-start = ((), (), s32[]{:S(2)}) async-start(), calls=%async_computation.3 | async-start | bytes 8650752
  225.0 316.7 %copy-start.16 = (s32[512]{0:T(512)S(1)}, s32[512]{0:T(512)}, u32[]{:S(2)}) copy-start(s32[512]{0:T(512)} %copy-done.15) | copy-start | bytes 6148
  (104 other events, 275.7 us)
Sparse Core Ops, SparseCore 0:
  220.0 76.8 reduce-scatter.6
  301.5 238.9 reduce-scatter.8
where the time goes:
time: 558 us; the launch traced here: 553 us
  waiting for transfers between devices  314 us (56%)
  blocking collectives  95.9 us (17%)
  local copies, waits for them, and re-layouts  62 us (11%)
  other arithmetic  33.4 us (6%)
  matrix products  30.4 us (5%)
  between operations  14.3 us (3%)
    unnamed x4, waiting for transfers between devices  314 us
    all_gather x1, blocking collectives, body(): j_all = lax.all_gather(packed, 'row', axis=1, tiled=True)  72.8 us
    all_gather x1, blocking collectives, body(): i_all = lax.all_gather(packed, 'col', axis=1, tiled=True)  23.2 us
    dot_general x9, matrix products, pair_forces(): coef6 = jnp.einsum('kba,kbc->bac', i_table6, j_onehot, precision=HIGH)  19.8 us
    gather x9, local copies, waits for them, and re-layouts, step(): jnp.take(i_tab6, i_sel, axis=1)  15.2 us
    unnamed x28, local copies, waits for them, and re-layouts  13 us
  transfers between devices with their start and end apart: 2, of which 2 were waited for; matrix products, arithmetic and copies ran while one was open for 1% of the time, Pallas kernels for 0%

commit v1 on v0

v1 whole, which is shorter than its diff:
```python
import functools

import jax
import jax.numpy as jnp
import numpy as np
from jax import lax
from jax.experimental import pallas as pl
from jax.experimental.pallas import tpu as pltpu
from jax.sharding import PartitionSpec as P

F32 = jnp.float32
BF16 = jnp.bfloat16
I32 = jnp.int32
MESH = pl.DeviceIdType.MESH
HIGH = lax.Precision.HIGHEST

BLOCK = 128
BPD = 4
GROUP = BPD * BLOCK
N_ROW = 32
N_COL = 16
NTYPE = 18
TYPE_PAD = 24
SOFT_CORE = 0.25
CUT_SQ = 1.2 * 1.2
CELL_SIDE = 2.47
KICK_FACTOR = 0.02 / 72.0

GRID = 2.46875
WRAP_X = float(np.float32(N_COL * CELL_SIDE) - np.float32(N_COL * GRID))
WRAP_Y = float(np.float32(N_ROW * CELL_SIDE) - np.float32(N_ROW * GRID))

CUT_X = float(np.float32(CUT_SQ + SOFT_CORE))
FEATURES = 32 + 2 * TYPE_PAD
LINK = GROUP + 2 * BLOCK
GROUPS = (
    (0, 0, 0, 256),
    (0, 1, 0, 256),
    (0, 2, 128, 256),
    (1, 1, 256, 384),
    (1, 2, 256, 512),
    (1, 3, 256, 512),
)
NT = (((1,), (1,)), ((), ()))


def iota(shape, dim):
    return lax.broadcasted_iota(I32, shape, dim)


def split3(x):
    high = x.astype(BF16).astype(F32)
    rest = x - high
    mid = rest.astype(BF16).astype(F32)
    return high, mid, rest - mid


def kernel(
    pos_ref, typ_ref, slot_ref, pair_ref, count_ref, c6_ref, c12_ref, out_ref,
    rec, perm, stage, pairs, tab, lhs_w, lhs_6, lhs_12, own_z, expand, acc,
    send_sem, recv_sem,
):
    row, col = lax.axis_index("row"), lax.axis_index("col")
    u = 2 * (col % 8) + col // 8
    v = 2 * (row % 16) + row // 16

    def device_at(e, f):
        to_u = (u + e + N_COL) % N_COL
        to_v = (v + f + N_ROW) % N_ROW
        return (to_v // 2 + to_v % 2 * 16, to_u // 2 + to_u % 2 * 8)

    around = [(e, f) for f in (-1, 0, 1) for e in (-1, 0, 1) if (e, f) != (0, 0)]

    def slot_of(e, f):
        return (f + 1) * 3 + e + 1

    barrier = pltpu.get_barrier_semaphore()
    for e, f in around:
        pl.semaphore_signal(barrier, inc=1, device_id=device_at(e, f), device_id_type=MESH)

    perm[...] = (iota((GROUP, GROUP), 0) == slot_ref[...]).astype(F32).astype(BF16)
    stage[...] = jnp.zeros_like(stage)
    stage[0:3, :] = pos_ref[...]
    stage[3:4, :] = typ_ref[...].astype(F32)
    which = iota((8, GROUP), 0)
    lane = iota((8, GROUP), 1)
    layer = lane // BLOCK
    half = GRID * 0.5
    origin = jnp.where(which == 0, u.astype(F32) * GRID + half, 0.0)
    origin = jnp.where(which == 1, v.astype(F32) * GRID + half, origin)
    parts = jnp.concatenate(split3(stage[...] - origin), axis=0).astype(BF16)
    moved = jnp.dot(parts, perm[...], preferred_element_type=F32)
    own = moved[0:8] + moved[8:16] + moved[16:24]
    own = own - jnp.where(which == 2, layer.astype(F32) * GRID + half, 0.0)
    rec[4, :, 0:GROUP] = own[0:4]

    pairs[...] = jnp.zeros_like(pairs)
    pairs[0:2, 0:72] = pair_ref[...]
    code = pairs[...]
    first, second = code[0:1], code[1:2]
    at_a = 2 * ((first >> 2) & 7) + (first >> 5)
    at_b = 2 * ((second >> 2) & 15) + (second >> 6)
    du = (at_a - u + 1) & (N_COL - 1)
    dv = (at_b - v + 1) & (N_ROW - 1)
    ka, kb = first & 3, second & 3
    live = iota((1, BLOCK), 1) < count_ref[0]
    eight = iota((8, BLOCK), 0)
    full = iota((BLOCK, BLOCK), 0)

    def table(layer_at, at):
        left = jnp.where((eight == layer_at) & live, 1.0, 0.0).astype(BF16)
        right = jnp.where(full == at, 1.0, 0.0).astype(BF16)
        return lax.dot_general(left, right, NT, preferred_element_type=F32)

    rec[4, :, GROUP : GROUP + BLOCK] = table(ka, du * 16 + dv * 4 + kb)[0:4]
    rec[4, :, GROUP + BLOCK : LINK] = table(kb, dv * 16 + du * 4 + ka)[0:4]

    pl.semaphore_wait(barrier, 8)
    copies = []
    for e, f in around:
        width = GROUP if e and f else LINK
        copy = pltpu.make_async_remote_copy(
            src_ref=rec.at[4, :, pl.ds(0, width)],
            dst_ref=rec.at[slot_of(-e, -f), :, pl.ds(0, width)],
            send_sem=send_sem.at[slot_of(e, f)],
            recv_sem=recv_sem.at[slot_of(-e, -f)],
            device_id=device_at(e, f),
            device_id_type=MESH,
        )
        copy.start()
        copies.append(copy)

    row4 = which & 3
    upper = which < 4
    own8 = jnp.concatenate([own[0:4], own[0:4]], axis=0)
    zeros = jnp.zeros((2 * TYPE_PAD, BLOCK), F32)
    for a, (p, k, _, _) in enumerate(GROUPS):
        at = slice(k * BLOCK, (k + 1) * BLOCK)
        pick, low = row4[:, at], upper[:, at]
        x = own8[:, at] + jnp.where(pick == 2, (k - 2 * p - 0.5) * GRID, 0.0)
        own_z[a] = x
        x = jnp.where(pick == 3, 0.0, x)
        norm = jnp.sum(x[0:4] * x[0:4], axis=0, keepdims=True) + SOFT_CORE
        h, m, l = split3(x)
        one = jnp.where(pick == 3, 1.0, 0.0)
        nh, nm, nl = split3(norm)
        kind = which[:, at]
        sides = [
            -2.0 * h + one,
            -2.0 * jnp.where(low, m, h) + jnp.where(low, 0.0, one),
            -2.0 * jnp.where(low, l, m),
            jnp.where(kind == 0, nh, jnp.where(kind == 1, nm, jnp.where(kind == 2, nl, 0.0))),
            zeros,
        ]
        lhs_w[a] = jnp.concatenate(sides, axis=0).T.astype(BF16)

    kinds = (iota((TYPE_PAD, GROUP), 0).astype(F32) == own[3:4]).astype(F32)
    blank = jnp.zeros((32, BLOCK), F32)
    for source, target, factor in ((c6_ref, lhs_6, 6.0), (c12_ref, lhs_12, 12.0)):
        tab[...] = jnp.zeros_like(tab)
        tab[0:NTYPE, 0:NTYPE] = source[...] * factor
        coef = jnp.dot(tab[:, 0:TYPE_PAD], kinds, precision=HIGH, preferred_element_type=F32)
        high = coef.astype(BF16).astype(F32)
        low = coef - high
        for k in range(BPD):
            at = slice(k * BLOCK, (k + 1) * BLOCK)
            side = jnp.concatenate([blank, high[:, at], low[:, at]], axis=0)
            target[k] = side.T.astype(BF16)
    expand[...] = (iota((16, GROUP), 0) == iota((16, GROUP), 1) // BLOCK).astype(F32).astype(BF16)
    acc[...] = jnp.zeros_like(acc)

    inv_cut = 1.0 / (CUT_X)
    cut4 = inv_cut**4
    cut7 = inv_cut**7

    def column(t, carry):
        corner = t // 5
        own_turn = (8 - t) // 8
        slot = (
            own_turn * 4
            + (1 - corner) * (1 - own_turn) * (2 * t - 1)
            + corner * (2 * (t - 5) + 2 * ((t + 1) // 2 - 3))
        )
        e, f = slot % 3 - 1, slot // 3 - 1

        @pl.when(t > 0)
        def _():
            @pl.when(t < 5)
            def _():
                pltpu.make_async_remote_copy(
                    src_ref=rec.at[4], dst_ref=rec.at[slot],
                    send_sem=send_sem.at[slot], recv_sem=recv_sem.at[slot],
                    device_id=device_at(e, f), device_id_type=MESH,
                ).wait_recv()

            @pl.when(t >= 5)
            def _():
                pltpu.make_async_remote_copy(
                    src_ref=rec.at[4, :, pl.ds(0, GROUP)],
                    dst_ref=rec.at[slot, :, pl.ds(0, GROUP)],
                    send_sem=send_sem.at[slot], recv_sem=recv_sem.at[slot],
                    device_id=device_at(e, f), device_id_type=MESH,
                ).wait_recv()

        tab_u = rec[3 + e + 1, :, GROUP : GROUP + BLOCK]
        tab_v = rec[(f + 1) * 3 + 1, :, GROUP + BLOCK : LINK]
        shift_u = BLOCK - ((1 - e) * 16 + (1 + f) * 4)
        shift_v = BLOCK - ((1 - f) * 16 + (1 + e) * 4)
        tab_u = pltpu.roll(jnp.concatenate([tab_u, tab_u], axis=0), shift_u, 1)
        tab_v = pltpu.roll(jnp.concatenate([tab_v, tab_v], axis=0), shift_v, 1)
        seen = (tab_u + tab_v)[:, 0:16]
        weight = jnp.dot(seen.astype(BF16), expand[...], preferred_element_type=F32)
        twice = jnp.where((slot == 4) & (which == layer), 0.5, 1.0)
        weight = weight * twice

        beads = rec[slot, :, 0:GROUP]
        beads = jnp.concatenate([beads, beads], axis=0)
        over_u = (u + e + N_COL) // N_COL - 1
        over_v = (v + f + N_ROW) // N_ROW - 1
        shift_x = e.astype(F32) * GRID + over_u.astype(F32) * WRAP_X
        shift_y = f.astype(F32) * GRID + over_v.astype(F32) * WRAP_Y
        shift_z = ((layer & 1).astype(F32) - 0.5) * GRID
        shift = jnp.where(row4 == 0, shift_x, jnp.where(row4 == 1, shift_y, shift_z))
        x = jnp.where(row4 == 3, 0.0, beads + shift)
        norm = jnp.sum(x[0:4] * x[0:4], axis=0, keepdims=True)
        h, m, l = split3(jnp.where(row4 == 3, norm, x))
        high_mid = jnp.where(upper, h, m)
        kind_row = iota((TYPE_PAD, GROUP), 0).astype(F32)
        onehot = (kind_row == beads[3:4]).astype(F32)
        rhs = jnp.concatenate(
            [high_mid, jnp.where(upper, h, l), high_mid, jnp.ones((8, GROUP), F32), onehot, onehot],
            axis=0,
        ).astype(BF16)
        back = jnp.concatenate([high_mid, jnp.where(upper, l, 1.0)], axis=0)

        for a, (p, k, start, stop) in enumerate(GROUPS):
            side = rhs[:, start:stop]
            dist = jnp.dot(lhs_w[a], side, preferred_element_type=F32)
            c6 = jnp.dot(lhs_6[k], side, preferred_element_type=F32)
            c12 = jnp.dot(lhs_12[k], side, preferred_element_type=F32)
            inv = 1.0 / jnp.minimum(dist, CUT_X)
            inv2 = inv * inv
            inv3 = inv2 * inv
            inv4 = inv2 * inv2
            scalar = c12 * (inv4 * inv3 - cut7) - c6 * (inv4 - cut4)
            high = scalar.astype(BF16)
            low = (scalar - high.astype(F32)).astype(BF16)
            pull = (back[:, start:stop] * weight[k : k + 1, start:stop]).astype(BF16)
            acc[a] += lax.dot_general(pull, high, NT, preferred_element_type=F32) + lax.dot_general(
                pull, low, NT, preferred_element_type=F32
            )
        return carry

    lax.fori_loop(0, 9, column, 0)

    force = []
    for k in range(BPD):
        total = jnp.zeros((8, BLOCK), F32)
        for a, group in enumerate(GROUPS):
            if group[1] == k:
                got = acc[a]
                pulled = got[0:8] + pltpu.roll(got[0:8], 4, 0) + got[8:16]
                total += own_z[a] * got[12:13] - pulled
        force.append(total)
    force = jnp.concatenate(force, axis=1) * KICK_FACTOR
    parts = jnp.concatenate(split3(force), axis=0).astype(BF16)
    stored = lax.dot_general(parts, perm[...], NT, preferred_element_type=F32)
    out_ref[...] = (stored[0:8] + stored[8:16] + stored[16:24])[0:3]

    for copy in copies:
        copy.wait_send()


def body(positions, velocities, bead_types, slot_bead, tile_pairs, tile_count, c6_table, c12_table):
    vmem = pl.BlockSpec(memory_space=pltpu.VMEM)
    smem = pl.BlockSpec(memory_space=pltpu.SMEM)
    kick = pl.pallas_call(
        kernel,
        out_shape=jax.ShapeDtypeStruct((3, GROUP), F32),
        in_specs=[vmem, vmem, vmem, vmem, smem, vmem, vmem],
        out_specs=vmem,
        scratch_shapes=[
            pltpu.VMEM((9, 4, LINK), F32),
            pltpu.VMEM((GROUP, GROUP), BF16),
            pltpu.VMEM((8, GROUP), F32),
            pltpu.VMEM((8, BLOCK), I32),
            pltpu.VMEM((TYPE_PAD, BLOCK), F32),
            pltpu.VMEM((6, BLOCK, FEATURES), BF16),
            pltpu.VMEM((4, BLOCK, FEATURES), BF16),
            pltpu.VMEM((4, BLOCK, FEATURES), BF16),
            pltpu.VMEM((6, 8, BLOCK), F32),
            pltpu.VMEM((16, GROUP), BF16),
            pltpu.VMEM((6, 16, BLOCK), F32),
            pltpu.SemaphoreType.DMA((9,)),
            pltpu.SemaphoreType.DMA((9,)),
        ],
        compiler_params=pltpu.CompilerParams(
            collective_id=0, has_side_effects=True, vmem_limit_bytes=48 * 2**20
        ),
        name="column_forces",
    )(
        positions,
        bead_types.reshape(1, GROUP),
        slot_bead.reshape(1, GROUP),
        tile_pairs,
        tile_count,
        c6_table,
        c12_table,
    )
    return velocities + kick


def solution(mesh):
    return jax.shard_map(
        body,
        mesh=mesh,
        in_specs=(
            P(None, ("row", "col")),
            P(None, ("row", "col")),
            P(("row", "col")),
            P(("row", "col")),
            P(None, ("row", "col")),
            P(("row", "col")),
            P(),
            P(),
        ),
        out_specs=P(None, ("row", "col")),
        check_vma=False,
    )
```

time: 558 us -> 37.6 us (0.07)
  waiting for transfers between devices: 314 us -> 0 us
  blocking collectives: 95.9 us -> 0 us
  local copies, waits for them, and re-layouts: 62 us -> 2.79 us
  Pallas kernels: 0 us -> 33.1 us
  other arithmetic: 33.4 us -> 0.6 us
  matrix products: 30.4 us -> 0 us
  between operations: 14.3 us -> 0.71 us
    unnamed x4 -> x0, waiting for transfers between devices: 314 us -> none
    all_gather x2 -> x0, blocking collectives: 95.9 us -> none  [the longest x1 72.8 us: body(): j_all = lax.all_gather(packed, 'row', axis=1, tiled=True)]
    gather x47 -> x0, local copies, waits for them, and re-layouts: 40.2 us -> none  [the longest x9 15.2 us: step(): jnp.take(i_tab6, i_sel, axis=1)]
    pallas_call x0 -> x1, Pallas kernels: none -> 33.1 us  [body(): pl.pallas_call(kernel, out_shape=jax.ShapeDtypeStruct((3, GROUP), F32), i...]
    dot_general x20 -> x0, matrix products: 30.4 us -> none  [the longest x9 19.8 us: pair_forces(): coef6 = jnp.einsum('kba,kbc->bac', i_table6, j_onehot, precision=HIGH)]
    scatter-add x19 -> x0, other arithmetic: 17.6 us -> none  [the longest x9 7.05 us: step(): carry[0].at[:, i_sel].add(force_i)]
    unnamed x28 -> x14, local copies, waits for them, and re-layouts: 13 us -> 2.79 us
    mul x19 -> x0, local copies, waits for them, and re-layouts: 6.57 us -> none  [the longest x9 6.33 us: pair_forces(): jnp.where(dist_sq < CUT_OFF * CUT_OFF, scalar, 0.0) * live[:, None, None]]
  transfers between devices with their start and end apart: 2 -> 0, of which waited for: 2 -> 0; matrix products, arithmetic and copies ran while one was open for 1% -> 0% of each run, Pallas kernels for 0% -> 0%
where the time goes in v1:
time: 37.6 us; the launch traced here: 37.2 us
  Pallas kernels  33.1 us (88%)
  local copies, waits for them, and re-layouts  2.79 us (7%)
  between operations  0.71 us (2%)
  other arithmetic  0.6 us (2%)
    pallas_call x1, Pallas kernels, body(): pl.pallas_call(kernel, out_shape=jax.ShapeDtypeStruct((3, GROUP), F32), i...  33.1 us
    unnamed x14, local copies, waits for them, and re-layouts  2.79 us

profile of v1, /device:TPU:1, one launch (start us, length us, event | category | flops | bytes accessed | tf_op | source)
XLA Modules:
  0.0 37.2 jit_solution(9522104776798353486)
XLA Ops:
  0.0 0.0 copy-start.4
  0.7 0.0 copy-start.3
  0.7 0.0 copy-start.5
  0.7 0.0 copy-done.4
  0.7 0.7 %copy-done.3 = s32[512]{0:T(512)S(1)} copy-done((s32[512]{0:T(512)S(1)}, s32[512]{0:T(512)}, u32[]{:S(2)}) %copy-start.3) | copy-done | bytes 2072
  1.4 0.0 copy-done.5
  1.4 0.0 copy-start
  1.4 0.7 %copy-done = f32[18,18]{1,0:T(8,128)S(1)} copy-done((f32[18,18]{1,0:T(8,128)S(1)}, f32[18,18]{1,0:T(8,128)}, u32[]{:S(2)}) %copy-start) | copy-done | bytes 1320
  2.1 0.0 copy-start.1
  2.1 0.7 %copy-done.1 = f32[18,18]{1,0:T(8,128)S(1)} copy-done((f32[18,18]{1,0:T(8,128)S(1)}, f32[18,18]{1,0:T(8,128)}, u32[]{:S(2)}) %copy-start.1) | copy-done | bytes 1320
  2.8 0.0 copy-start.2
  2.8 0.7 %copy-done.2 = f32[3,512]{1,0:T(4,128)S(1)} copy-done((f32[3,512]{1,0:T(4,128)S(1)}, f32[3,512]{1,0:T(4,128)}, u32[]{:S(2)}) %copy-start.2) | copy-done | bytes 6168
  3.5 0.0 copy-start.6
  3.5 33.1 %column_forces.1 = f32[3,512]{1,0:T(4,128)S(1)} custom-call(f32[3,512]{1,0:T(4,128)S(1)} %copy-done.2, s32[1,512]{1,0:T(1,128)S(1)} %bitcast.2, s32[1,512]{1,0:T(1,128)S(1)} %bitcast.3, s32[2,72]{1,0:T(2,128)S(1)} %copy-done.5, s32[1]{0:T(128)S(6)} %copy.9.count_ref, f32[18,18]{1,0:T(8,128)S(1)} %copy-done, f32[18,18]{1,0:T(8,128)S(1)} %copy-done.1), custom_call_target="tpu_custom_call" | custom-call | tf_op jit(solution)/shard_map/column_forces/pallas_call | solution.py:277
  36.6 0.0 copy-done.6
  36.6 0.6 %add.3 = f32[3,512]{1,0:T(4,128)} add(f32[3,512]{1,0:T(4,128)S(1)} %copy-done.6, f32[3,512]{1,0:T(4,128)S(1)} %column_forces.1) | non-fusion elementwise | flops 1536 | bytes 18432 | tf_op jit(solution)/shard_map/add | solution.py:310
Async XLA Ops:
  0.0 0.7 %copy-start.4 = (s32[512]{0:T(512)S(1)}, s32[512]{0:T(512)}, u32[]{:S(2)}) copy-start(s32[512]{0:T(512)} %param.11) | copy-start | bytes 6148
  0.7 0.7 %copy-start.3 = (s32[512]{0:T(512)S(1)}, s32[512]{0:T(512)}, u32[]{:S(2)}) copy-start(s32[512]{0:T(512)} %param.10) | copy-start | bytes 6148
  0.7 0.7 %copy-start.5 = (s32[2,72]{1,0:T(2,128)S(1)}, s32[2,72]{1,0:T(2,128)}, u32[]{:S(2)}) copy-start(s32[2,72]{1,0:T(2,128)} %pair_ref.1) | copy-start | bytes 1732
  1.4 0.7 %copy-start = (f32[18,18]{1,0:T(8,128)S(1)}, f32[18,18]{1,0:T(8,128)}, u32[]{:S(2)}) copy-start(f32[18,18]{1,0:T(8,128)} %c6_ref.1) | copy-start | bytes 3892
  2.1 0.7 %copy-start.1 = (f32[18,18]{1,0:T(8,128)S(1)}, f32[18,18]{1,0:T(8,128)}, u32[]{:S(2)}) copy-start(f32[18,18]{1,0:T(8,128)} %c12_ref.1) | copy-start | bytes 3892
  2.8 0.7 %copy-start.2 = (f32[3,512]{1,0:T(4,128)S(1)}, f32[3,512]{1,0:T(4,128)}, u32[]{:S(2)}) copy-start(f32[3,512]{1,0:T(4,128)} %pos_ref.1) | copy-start | bytes 18436
  3.5 33.1 %copy-start.6 = (f32[3,512]{1,0:T(4,128)S(1)}, f32[3,512]{1,0:T(4,128)}, u32[]{:S(2)}) copy-start(f32[3,512]{1,0:T(4,128)} %param.9) | copy-start | bytes 18436

commit v2 on v1

v2 whole, which is shorter than its diff:
```python
import functools

import jax
import jax.numpy as jnp
import numpy as np
from jax import lax
from jax.experimental import pallas as pl
from jax.experimental.pallas import tpu as pltpu
from jax.sharding import PartitionSpec as P

F32 = jnp.float32
BF16 = jnp.bfloat16
I32 = jnp.int32
MESH = pl.DeviceIdType.MESH
HIGH = lax.Precision.HIGHEST

BLOCK = 128
BPD = 4
GROUP = BPD * BLOCK
N_ROW = 32
N_COL = 16
NTYPE = 18
TYPE_PAD = 24
SOFT_CORE = 0.25
CUT_SQ = 1.2 * 1.2
CELL_SIDE = 2.47
KICK_FACTOR = 0.02 / 72.0

GRID = 2.46875
WRAP_X = float(np.float32(N_COL * CELL_SIDE) - np.float32(N_COL * GRID))
WRAP_Y = float(np.float32(N_ROW * CELL_SIDE) - np.float32(N_ROW * GRID))

CUT_X = float(np.float32(CUT_SQ + SOFT_CORE))
FEATURES = 32 + 2 * TYPE_PAD
LINK = GROUP + 2 * BLOCK
GROUPS = (
    (0, 0, 256, 0, 256),
    (0, 256, 384, 128, 256),
    (1, 128, 256, 256, 384),
    (1, 256, 512, 256, 512),
)
CHUNK = 64
NT = (((1,), (1,)), ((), ()))


def iota(shape, dim):
    return lax.broadcasted_iota(I32, shape, dim)


def split3(x):
    high = x.astype(BF16).astype(F32)
    rest = x - high
    mid = rest.astype(BF16).astype(F32)
    return high, mid, rest - mid


def kernel(
    pos_hbm, typ_hbm, slot_hbm, pair_hbm, count_hbm, c6_hbm, c12_hbm, out_ref,
    pos_ref, typ_ref, slot_ref, pair_ref, count_ref, c6_ref, c12_ref,
    rec, perm, stage, pairs, tab, rhs_w, rhs_6, rhs_12, own_z, expand, feat, high, low, acc,
    load_sem, send_sem, recv_sem,
):
    loads = [
        pltpu.make_async_copy(source, target, load_sem.at[n])
        for n, (source, target) in enumerate((
            (slot_hbm, slot_ref), (pos_hbm, pos_ref), (typ_hbm, typ_ref), (pair_hbm, pair_ref),
            (count_hbm, count_ref), (c6_hbm, c6_ref), (c12_hbm, c12_ref),
        ))
    ]
    for load in loads:
        load.start()
    row, col = lax.axis_index("row"), lax.axis_index("col")
    u = 2 * (col % 8) + col // 8
    v = 2 * (row % 16) + row // 16

    def device_at(e, f):
        to_u = (u + e + N_COL) % N_COL
        to_v = (v + f + N_ROW) % N_ROW
        return (to_v // 2 + to_v % 2 * 16, to_u // 2 + to_u % 2 * 8)

    around = [(e, f) for f in (-1, 0, 1) for e in (-1, 0, 1) if (e, f) != (0, 0)]

    def slot_of(e, f):
        return (f + 1) * 3 + e + 1

    barrier = pltpu.get_barrier_semaphore()
    for e, f in around:
        pl.semaphore_signal(barrier, inc=1, device_id=device_at(e, f), device_id_type=MESH)

    for load in loads:
        load.wait()

    perm[...] = (iota((GROUP, GROUP), 0) == slot_ref[...]).astype(F32).astype(BF16)
    stage[...] = jnp.zeros_like(stage)
    stage[0:3, :] = pos_ref[...]
    stage[3:4, :] = typ_ref[...].astype(F32)
    which = iota((8, GROUP), 0)
    lane = iota((8, GROUP), 1)
    layer = lane // BLOCK
    half = GRID * 0.5
    origin = jnp.where(which == 0, u.astype(F32) * GRID + half, 0.0)
    origin = jnp.where(which == 1, v.astype(F32) * GRID + half, origin)
    parts = jnp.concatenate(split3(stage[...] - origin), axis=0).astype(BF16)
    moved = jnp.dot(parts, perm[...], preferred_element_type=F32)
    own = moved[0:8] + moved[8:16] + moved[16:24]
    own = own - jnp.where(which == 2, layer.astype(F32) * GRID + half, 0.0)
    rec[4, :, 0:GROUP] = own[0:4]

    pairs[...] = jnp.zeros_like(pairs)
    pairs[0:2, 0:72] = pair_ref[...]
    code = pairs[...]
    first, second = code[0:1], code[1:2]
    at_a = 2 * ((first >> 2) & 7) + (first >> 5)
    at_b = 2 * ((second >> 2) & 15) + (second >> 6)
    du = (at_a - u + 1) & (N_COL - 1)
    dv = (at_b - v + 1) & (N_ROW - 1)
    ka, kb = first & 3, second & 3
    live = iota((1, BLOCK), 1) < count_ref[0]
    eight = iota((8, BLOCK), 0)
    full = iota((BLOCK, BLOCK), 0)

    def table(layer_at, at):
        left = jnp.where((eight == layer_at) & live, 1.0, 0.0).astype(BF16)
        right = jnp.where(full == at, 1.0, 0.0).astype(BF16)
        return lax.dot_general(left, right, NT, preferred_element_type=F32)

    rec[4, :, GROUP : GROUP + BLOCK] = table(ka, du * 16 + dv * 4 + kb)[0:4]
    rec[4, :, GROUP + BLOCK : LINK] = table(kb, dv * 16 + du * 4 + ka)[0:4]

    pl.semaphore_wait(barrier, 8)
    copies = []
    for e, f in around:
        width = GROUP if e and f else LINK
        copy = pltpu.make_async_remote_copy(
            src_ref=rec.at[4, :, pl.ds(0, width)],
            dst_ref=rec.at[slot_of(-e, -f), :, pl.ds(0, width)],
            send_sem=send_sem.at[slot_of(e, f)],
            recv_sem=recv_sem.at[slot_of(-e, -f)],
            device_id=device_at(e, f),
            device_id_type=MESH,
        )
        copy.start()
        copies.append(copy)

    row4 = which & 3
    upper = which < 4
    own8 = jnp.concatenate([own[0:4], own[0:4]], axis=0)
    one = jnp.where(row4 == 3, 1.0, 0.0)
    zeros = jnp.zeros((2 * TYPE_PAD, GROUP), F32)
    for p in range(2):
        x = own8 + jnp.where(row4 == 2, (layer.astype(F32) - (2 * p + 0.5)) * GRID, 0.0)
        x = jnp.where(row4 == 3, 0.0, x)
        own_z[p] = x
        norm = jnp.sum(x[0:4] * x[0:4], axis=0, keepdims=True) + SOFT_CORE
        h, m, l = split3(x)
        nh, nm, nl = split3(norm)
        sides = [
            -2.0 * h + one,
            -2.0 * jnp.where(upper, m, h) + jnp.where(upper, 0.0, one),
            -2.0 * jnp.where(upper, l, m),
            jnp.where(which == 0, nh, jnp.where(which == 1, nm, jnp.where(which == 2, nl, 0.0))),
            zeros,
        ]
        rhs_w[p] = jnp.concatenate(sides, axis=0).astype(BF16)

    kinds = (iota((TYPE_PAD, GROUP), 0).astype(F32) == own[3:4]).astype(F32)
    blank = jnp.zeros((32, GROUP), F32)
    for source, target, factor in ((c6_ref, rhs_6, 6.0), (c12_ref, rhs_12, 12.0)):
        tab[...] = jnp.zeros_like(tab)
        tab[0:NTYPE, 0:NTYPE] = source[...] * factor
        coef = jnp.dot(tab[:, 0:TYPE_PAD], kinds, precision=HIGH, preferred_element_type=F32)
        first_part = coef.astype(BF16).astype(F32)
        target[...] = jnp.concatenate([blank, first_part, coef - first_part], axis=0).astype(BF16)
    expand[...] = (iota((16, GROUP), 0) == iota((16, GROUP), 1) // BLOCK).astype(F32).astype(BF16)
    acc[...] = jnp.zeros_like(acc)

    inv_cut = 1.0 / (CUT_X)
    cut4 = inv_cut**4
    cut7 = inv_cut**7

    ahead = 1 - 2 * (v % 2)

    def wait(slot, width):
        pltpu.make_async_remote_copy(
            src_ref=rec.at[4, :, pl.ds(0, width)],
            dst_ref=rec.at[slot, :, pl.ds(0, width)],
            send_sem=send_sem.at[slot], recv_sem=recv_sem.at[slot],
            device_id=device_at(1, 0), device_id_type=MESH,
        ).wait_recv()

    def features(slot, at, scale):
        e, f = slot % 3 - 1, slot // 3 - 1
        tab_u = rec[3 + e + 1, :, GROUP : GROUP + BLOCK]
        tab_v = rec[(f + 1) * 3 + 1, :, GROUP + BLOCK : LINK]
        shift_u = BLOCK - ((1 - e) * 16 + (1 + f) * 4)
        shift_v = BLOCK - ((1 - f) * 16 + (1 + e) * 4)
        tab_u = pltpu.roll(jnp.concatenate([tab_u, tab_u], axis=0), shift_u, 1)
        tab_v = pltpu.roll(jnp.concatenate([tab_v, tab_v], axis=0), shift_v, 1)
        seen = (tab_u + tab_v)[:, 0:16]
        weight = jnp.dot(seen.astype(BF16), expand[...], preferred_element_type=F32)
        twice = jnp.where((slot == 4) & (which == layer), 0.5, 1.0)
        weight = weight * twice * scale

        beads = rec[slot, :, 0:GROUP]
        beads = jnp.concatenate([beads, beads], axis=0)
        over_u = (u + e + N_COL) // N_COL - 1
        over_v = (v + f + N_ROW) // N_ROW - 1
        shift_x = e.astype(F32) * GRID + over_u.astype(F32) * WRAP_X
        shift_y = f.astype(F32) * GRID + over_v.astype(F32) * WRAP_Y
        shift_z = ((layer & 1).astype(F32) - 0.5) * GRID
        shift = jnp.where(row4 == 0, shift_x, jnp.where(row4 == 1, shift_y, shift_z))
        x = jnp.where(row4 == 3, 0.0, beads + shift)
        norm = jnp.sum(x[0:4] * x[0:4], axis=0, keepdims=True)
        h, m, l = split3(jnp.where(row4 == 3, norm, x))
        high_mid = jnp.where(upper, h, m)
        kind_row = iota((TYPE_PAD, GROUP), 0).astype(F32)
        onehot = (kind_row == beads[3:4]).astype(F32)
        rows = jnp.concatenate(
            [high_mid, jnp.where(upper, h, l), high_mid, jnp.ones((8, GROUP), F32), onehot, onehot],
            axis=0,
        )
        for k in range(BPD):
            feat[at, k * BLOCK : (k + 1) * BLOCK, :] = rows[:, k * BLOCK : (k + 1) * BLOCK].T.astype(BF16)
        back = jnp.concatenate([high_mid, jnp.where(upper, l, 1.0)], axis=0)
        return back, weight

    def scalars(at):
        for p, m0, m1, n0, n1 in GROUPS:
            for n in range(n0, n1, CHUNK):
                side = feat[at, n : n + CHUNK, :]
                dist = jnp.dot(side, rhs_w[p, :, m0:m1], preferred_element_type=F32)
                c6 = jnp.dot(side, rhs_6[:, m0:m1], preferred_element_type=F32)
                c12 = jnp.dot(side, rhs_12[:, m0:m1], preferred_element_type=F32)
                inv = 1.0 / jnp.minimum(dist, CUT_X)
                inv2 = inv * inv
                inv3 = inv2 * inv
                inv4 = inv2 * inv2
                scalar = c12 * (inv4 * inv3 - cut7) - c6 * (inv4 - cut4)
                rounded = scalar.astype(BF16)
                high[at, n : n + CHUNK, m0:m1] = rounded
                low[at, n : n + CHUNK, m0:m1] = (scalar - rounded.astype(F32)).astype(BF16)

    def sums(at, back, weight):
        for p, m0, m1, n0, n1 in GROUPS:
            layers = range(m0 // BLOCK, m1 // BLOCK)
            pull = jnp.concatenate(
                [back[:, n0:n1] * weight[k : k + 1, n0:n1] for k in layers], axis=0
            ).astype(BF16)
            got = jnp.dot(pull, high[at, n0:n1, m0:m1], preferred_element_type=F32) + jnp.dot(
                pull, low[at, n0:n1, m0:m1], preferred_element_type=F32
            )
            for n, k in enumerate(layers):
                lanes = slice(k * BLOCK, (k + 1) * BLOCK)
                acc[p, :, lanes] += got[16 * n : 16 * n + 16, n * BLOCK : (n + 1) * BLOCK]

    def two_columns(t, carry):
        is_u = (t == 1).astype(I32)
        is_far = (t == 2).astype(I32)
        is_side = (t == 3).astype(I32)
        is_near = (t == 4).astype(I32)
        e = is_u + is_far + is_near
        f = is_far * ahead - is_near * ahead
        one_slot = (f + is_side * ahead + 1) * 3 + 1 - e
        two_slot = (f - is_side * ahead + 1) * 3 + 1 + e

        @pl.when(is_u == 1)
        def _():
            wait(one_slot, LINK)
            wait(two_slot, LINK)

        @pl.when(is_far == 1)
        def _():
            wait((ahead + 1) * 3 + 1, LINK)

        @pl.when(is_side == 1)
        def _():
            wait((1 - ahead) * 3 + 1, LINK)

        @pl.when(is_far + is_near == 1)
        def _():
            wait(one_slot, GROUP)
            wait(two_slot, GROUP)

        scale = jnp.minimum(t, 1).astype(F32)
        first_side = features(one_slot, 0, 1.0)
        second_side = features(two_slot, 1, scale)
        scalars(0)
        scalars(1)
        sums(0, *first_side)
        sums(1, *second_side)
        return carry

    lax.fori_loop(0, 5, two_columns, 0)

    force = jnp.zeros((8, GROUP), F32)
    for p in range(2):
        got = acc[p]
        pulled = got[0:8] + pltpu.roll(got[0:8], 4, 0) + got[8:16]
        force += own_z[p] * got[12:13] - pulled
    force = force * KICK_FACTOR
    parts = jnp.concatenate(split3(force), axis=0).astype(BF16)
    stored = lax.dot_general(parts, perm[...], NT, preferred_element_type=F32)
    out_ref[...] = (stored[0:8] + stored[8:16] + stored[16:24])[0:3]

    for copy in copies:
        copy.wait_send()


def body(positions, velocities, bead_types, slot_bead, tile_pairs, tile_count, c6_table, c12_table):
    vmem = pl.BlockSpec(memory_space=pltpu.VMEM)
    hbm = pl.BlockSpec(memory_space=pltpu.HBM)
    kick = pl.pallas_call(
        kernel,
        out_shape=jax.ShapeDtypeStruct((3, GROUP), F32),
        in_specs=[hbm] * 7,
        out_specs=vmem,
        scratch_shapes=[
            pltpu.VMEM((3, GROUP), F32),
            pltpu.VMEM((1, GROUP), I32),
            pltpu.VMEM((1, GROUP), I32),
            pltpu.VMEM((2, 72), I32),
            pltpu.SMEM((1,), I32),
            pltpu.VMEM((NTYPE, NTYPE), F32),
            pltpu.VMEM((NTYPE, NTYPE), F32),
            pltpu.VMEM((9, 4, LINK), F32),
            pltpu.VMEM((GROUP, GROUP), BF16),
            pltpu.VMEM((8, GROUP), F32),
            pltpu.VMEM((8, BLOCK), I32),
            pltpu.VMEM((TYPE_PAD, BLOCK), F32),
            pltpu.VMEM((2, FEATURES, GROUP), BF16),
            pltpu.VMEM((FEATURES, GROUP), BF16),
            pltpu.VMEM((FEATURES, GROUP), BF16),
            pltpu.VMEM((2, 8, GROUP), F32),
            pltpu.VMEM((16, GROUP), BF16),
            pltpu.VMEM((2, GROUP, FEATURES), BF16),
            pltpu.VMEM((2, GROUP, GROUP), BF16),
            pltpu.VMEM((2, GROUP, GROUP), BF16),
            pltpu.VMEM((2, 16, GROUP), F32),
            pltpu.SemaphoreType.DMA((7,)),
            pltpu.SemaphoreType.DMA((9,)),
            pltpu.SemaphoreType.DMA((9,)),
        ],
        compiler_params=pltpu.CompilerParams(
            collective_id=0, has_side_effects=True, vmem_limit_bytes=60 * 2**20
        ),
        name="column_forces",
    )(
        positions,
        bead_types.reshape(1, GROUP),
        slot_bead.reshape(1, GROUP),
        tile_pairs,
        tile_count,
        c6_table,
        c12_table,
    )
    return velocities + kick


def solution(mesh):
    return jax.shard_map(
        body,
        mesh=mesh,
        in_specs=(
            P(None, ("row", "col")),
            P(None, ("row", "col")),
            P(("row", "col")),
            P(("row", "col")),
            P(None, ("row", "col")),
            P(("row", "col")),
            P(),
            P(),
        ),
        out_specs=P(None, ("row", "col")),
        check_vma=False,
    )
```

time: 37.6 us -> 27.9 us (0.74)
  Pallas kernels: 33.1 us -> 25.7 us
  local copies, waits for them, and re-layouts: 2.79 us -> 0.01 us
  other arithmetic: 0.6 us -> 1.3 us
    pallas_call x1, Pallas kernels: 33.1 us -> 25.7 us  [body(): pl.pallas_call(kernel, out_shape=jax.ShapeDtypeStruct((3, GROUP), F32), i...]
    unnamed x14 -> x2, local copies, waits for them, and re-layouts: 2.79 us -> 0.01 us
    add x1, other arithmetic: 0.6 us -> 1.3 us  [body(): return velocities + kick]
where the time goes in v2:
time: 27.9 us; the launch traced here: 27.7 us
  Pallas kernels  25.7 us (92%)
  other arithmetic  1.3 us (5%)
  between operations  0.68 us (2%)
    pallas_call x1, Pallas kernels, body(): pl.pallas_call(kernel, out_shape=jax.ShapeDtypeStruct((3, GROUP), F32), i...  25.7 us
    add x1, other arithmetic, body(): return velocities + kick  1.3 us

profile of v2, /device:TPU:1, one launch (start us, length us, event | category | flops | bytes accessed | tf_op | source)
XLA Modules:
  0.0 27.7 jit_solution(3524072013656984739)
XLA Ops:
  0.7 0.0 copy-start
  0.7 25.7 %column_forces.1 = f32[3,512]{1,0:T(4,128)} custom-call(f32[3,512]{1,0:T(4,128)} %pos_hbm.1, s32[1,512]{1,0:T(1,128)} %bitcast.2, s32[1,512]{1,0:T(1,128)} %bitcast.3, s32[2,72]{1,0:T(2,128)} %pair_hbm.1, s32[1]{0:T(128)S(6)} %copy.9.count_hbm, f32[18,18]{1,0:T(8,128)} %c6_hbm.1, f32[18,18]{1,0:T(8,128)} %c12_hbm.1), custom_call_target="tpu_custom_call" | custom-call | tf_op jit(solution)/shard_map/column_forces/pallas_call | solution.py:312
  26.3 0.0 copy-done
  26.4 1.3 %add.3 = f32[3,512]{1,0:T(4,128)} add(f32[3,512]{1,0:T(4,128)S(1)} %copy-done, f32[3,512]{1,0:T(4,128)} %column_forces.1) | non-fusion elementwise | flops 1536 | bytes 18432 | tf_op jit(solution)/shard_map/add | solution.py:356
Async XLA Ops:
  0.7 25.7 %copy-start = (f32[3,512]{1,0:T(4,128)S(1)}, f32[3,512]{1,0:T(4,128)}, u32[]{:S(2)}) copy-start(f32[3,512]{1,0:T(4,128)} %param.9) | copy-start | bytes 18436

commit v3 on v2

--- a/solution.py
+++ b/solution.py
@@ -83,9 +83,21 @@
     def slot_of(e, f):
         return (f + 1) * 3 + e + 1
 
+    early = v % 16 == 0
+    late = v % 16 == 15
     barrier = pltpu.get_barrier_semaphore()
+
+    def greet(e, f):
+        pl.semaphore_signal(barrier, inc=1, device_id=device_at(e, f), device_id_type=MESH)
+
     for e, f in around:
-        pl.semaphore_signal(barrier, inc=1, device_id=device_at(e, f), device_id_type=MESH)
+        if f < 1:
+            greet(e, f)
+
+    @pl.when(jnp.logical_not(late))
+    def _():
+        for e in (-1, 0, 1):
+            greet(e, 1)
 
     for load in loads:
         load.wait()
@@ -127,11 +139,9 @@
     rec[4, :, GROUP : GROUP + BLOCK] = table(ka, du * 16 + dv * 4 + kb)[0:4]
     rec[4, :, GROUP + BLOCK : LINK] = table(kb, dv * 16 + du * 4 + ka)[0:4]
 
-    pl.semaphore_wait(barrier, 8)
-    copies = []
-    for e, f in around:
+    def link(e, f):
         width = GROUP if e and f else LINK
-        copy = pltpu.make_async_remote_copy(
+        return pltpu.make_async_remote_copy(
             src_ref=rec.at[4, :, pl.ds(0, width)],
             dst_ref=rec.at[slot_of(-e, -f), :, pl.ds(0, width)],
             send_sem=send_sem.at[slot_of(e, f)],
@@ -139,8 +149,20 @@
             device_id=device_at(e, f),
             device_id_type=MESH,
         )
-        copy.start()
-        copies.append(copy)
+
+    @pl.when(early)
+    def _():
+        pl.semaphore_wait(barrier, 5)
+
+    @pl.when(jnp.logical_not(early))
+    def _():
+        pl.semaphore_wait(barrier, 8)
+        for e in (-1, 0, 1):
+            link(e, -1).start()
+
+    for e, f in around:
+        if f > -1:
+            link(e, f).start()
 
     row4 = which & 3
     upper = which < 4
@@ -276,10 +298,19 @@
         def _():
             wait((1 - ahead) * 3 + 1, LINK)
 
+            @pl.when(early)
+            def _():
+                link(0, -1).start()
+
         @pl.when(is_far + is_near == 1)
         def _():
             wait(one_slot, GROUP)
             wait(two_slot, GROUP)
+
+        @pl.when((is_near == 1) & early)
+        def _():
+            link(-1, -1).start()
+            link(1, -1).start()
 
         scale = jnp.minimum(t, 1).astype(F32)
         first_side = features(one_slot, 0, 1.0)
@@ -302,8 +333,8 @@
     stored = lax.dot_general(parts, perm[...], NT, preferred_element_type=F32)
     out_ref[...] = (stored[0:8] + stored[8:16] + stored[16:24])[0:3]
 
-    for copy in copies:
-        copy.wait_send()
+    for e, f in around:
+        link(e, f).wait_send()
 
 
 def body(positions, velocities, bead_types, slot_bead, tile_pairs, tile_count, c6_table, c12_table):
@@ -311,7 +342,7 @@
     hbm = pl.BlockSpec(memory_space=pltpu.HBM)
     kick = pl.pallas_call(
         kernel,
-        out_shape=jax.ShapeDtypeStruct((3, GROUP), F32),
+        out_shape=pltpu.VMEM((3, GROUP), F32),
         in_specs=[hbm] * 7,
         out_specs=vmem,
         scratch_shapes=[

time: 27.9 us -> 26 us (0.932)
  Pallas kernels: 25.7 us -> 24.5 us
  other arithmetic: 1.3 us -> 0.6 us
    pallas_call x1, Pallas kernels: 25.7 us -> 24.5 us  [body(): pl.pallas_call(kernel, out_shape=pltpu.VMEM((3, GROUP), F32), in_specs=[h...]
    add x1, other arithmetic: 1.3 us -> 0.6 us  [body(): return velocities + kick]
where the time goes in v3:
time: 26 us; the launch traced here: 25.8 us
  Pallas kernels  24.5 us (94%)
  between operations  0.68 us (3%)
  other arithmetic  0.6 us (2%)
    pallas_call x1, Pallas kernels, body(): pl.pallas_call(kernel, out_shape=pltpu.VMEM((3, GROUP), F32), in_specs=[h...  24.5 us
    add x1, other arithmetic, body(): return velocities + kick  0.6 us

profile of v3, /device:TPU:1, one launch (start us, length us, event | category | flops | bytes accessed | tf_op | source)
XLA Modules:
  0.0 25.8 jit_solution(13278201769634054439)
XLA Ops:
  0.7 0.0 copy-start
  0.7 24.5 %column_forces.1 = f32[3,512]{1,0:T(4,128)S(1)} custom-call(f32[3,512]{1,0:T(4,128)} %pos_hbm.1, s32[1,512]{1,0:T(1,128)} %bitcast.2, s32[1,512]{1,0:T(1,128)} %bitcast.3, s32[2,72]{1,0:T(2,128)} %pair_hbm.1, s32[1]{0:T(128)S(6)} %copy.9.count_hbm, f32[18,18]{1,0:T(8,128)} %c6_hbm.1, f32[18,18]{1,0:T(8,128)} %c12_hbm.1), custom_call_target="tpu_custom_call" | custom-call | tf_op jit(solution)/shard_map/column_forces/pallas_call | solution.py:343
  25.2 0.0 copy-done
  25.2 0.6 %add.3 = f32[3,512]{1,0:T(4,128)} add(f32[3,512]{1,0:T(4,128)S(1)} %copy-done, f32[3,512]{1,0:T(4,128)S(1)} %column_forces.1) | non-fusion elementwise | flops 1536 | bytes 18432 | tf_op jit(solution)/shard_map/add | solution.py:387
Async XLA Ops:
  0.7 24.5 %copy-start = (f32[3,512]{1,0:T(4,128)S(1)}, f32[3,512]{1,0:T(4,128)}, u32[]{:S(2)}) copy-start(f32[3,512]{1,0:T(4,128)} %param.9) | copy-start | bytes 18436

commit v4 on v3

--- a/solution.py
+++ b/solution.py
@@ -57,9 +57,54 @@
 def kernel(
     pos_hbm, typ_hbm, slot_hbm, pair_hbm, count_hbm, c6_hbm, c12_hbm, out_ref,
     pos_ref, typ_ref, slot_ref, pair_ref, count_ref, c6_ref, c12_ref,
-    rec, perm, stage, pairs, tab, rhs_w, rhs_6, rhs_12, own_z, expand, feat, high, low, acc,
+    rec, perm, unperm, stage, pairs, tab, rhs_w, rhs_6, rhs_12, own_z, expand, feat, high, low, acc,
     load_sem, send_sem, recv_sem,
 ):
+    row, col = lax.axis_index("row"), lax.axis_index("col")
+    u = 2 * (col % 8) + col // 8
+    v = 2 * (row % 16) + row // 16
+
+    def device_at(e, f):
+        to_u = (u + e + N_COL) % N_COL
+        to_v = (v + f + N_ROW) % N_ROW
+        return (to_v // 2 + to_v % 2 * 16, to_u // 2 + to_u % 2 * 8)
+
+    around = [(e, f) for f in (-1, 0, 1) for e in (-1, 0, 1) if (e, f) != (0, 0)]
+
+    def slot_of(e, f):
+        return (f + 1) * 3 + e + 1
+
+    early = v % 16 == 0
+    late = v % 16 == 15
+    below = v % 16 == 14
+    lower = v % 16 == 13
+    late_odd = late & (u % 2 == 1)
+    barrier = pltpu.get_barrier_semaphore()
+
+    def greet(e, f):
+        pl.semaphore_signal(barrier, inc=1, device_id=device_at(e, f), device_id_type=MESH)
+
+    greet(0, -1)
+
+    @pl.when(jnp.logical_not(late))
+    def _():
+        greet(-1, -1)
+        greet(1, -1)
+
+    @pl.when(jnp.logical_not(late | below))
+    def _():
+        greet(0, 1)
+
+    @pl.when(jnp.logical_not(late | below | lower))
+    def _():
+        greet(-1, 1)
+        greet(1, 1)
+
+    @pl.when(jnp.logical_not(late & (u % 2 == 0)))
+    def _():
+        greet(-1, 0)
+        greet(1, 0)
+
     loads = [
         pltpu.make_async_copy(source, target, load_sem.at[n])
         for n, (source, target) in enumerate((
@@ -69,36 +114,6 @@
     ]
     for load in loads:
         load.start()
-    row, col = lax.axis_index("row"), lax.axis_index("col")
-    u = 2 * (col % 8) + col // 8
-    v = 2 * (row % 16) + row // 16
-
-    def device_at(e, f):
-        to_u = (u + e + N_COL) % N_COL
-        to_v = (v + f + N_ROW) % N_ROW
-        return (to_v // 2 + to_v % 2 * 16, to_u // 2 + to_u % 2 * 8)
-
-    around = [(e, f) for f in (-1, 0, 1) for e in (-1, 0, 1) if (e, f) != (0, 0)]
-
-    def slot_of(e, f):
-        return (f + 1) * 3 + e + 1
-
-    early = v % 16 == 0
-    late = v % 16 == 15
-    barrier = pltpu.get_barrier_semaphore()
-
-    def greet(e, f):
-        pl.semaphore_signal(barrier, inc=1, device_id=device_at(e, f), device_id_type=MESH)
-
-    for e, f in around:
-        if f < 1:
-            greet(e, f)
-
-    @pl.when(jnp.logical_not(late))
-    def _():
-        for e in (-1, 0, 1):
-            greet(e, 1)
-
     for load in loads:
         load.wait()
 
@@ -150,19 +165,30 @@
             device_id_type=MESH,
         )
 
-    @pl.when(early)
-    def _():
-        pl.semaphore_wait(barrier, 5)
-
-    @pl.when(jnp.logical_not(early))
-    def _():
-        pl.semaphore_wait(barrier, 8)
-        for e in (-1, 0, 1):
-            link(e, -1).start()
-
-    for e, f in around:
-        if f > -1:
-            link(e, f).start()
+    count = lambda flag: flag.astype(I32)
+    expected = 8 - 3 * count(early) - 3 * count(late) - 2 * count(late_odd) - 4 * count(below)
+    pl.semaphore_wait(barrier, expected)
+
+    link(0, 1).start()
+
+    @pl.when(jnp.logical_not(below))
+    def _():
+        link(-1, 1).start()
+        link(1, 1).start()
+
+    @pl.when(jnp.logical_not(early | late))
+    def _():
+        link(0, -1).start()
+
+    @pl.when(jnp.logical_not(early | late | below))
+    def _():
+        link(-1, -1).start()
+        link(1, -1).start()
+
+    @pl.when(jnp.logical_not(late_odd))
+    def _():
+        link(-1, 0).start()
+        link(1, 0).start()
 
     row4 = which & 3
     upper = which < 4
@@ -193,6 +219,8 @@
         coef = jnp.dot(tab[:, 0:TYPE_PAD], kinds, precision=HIGH, preferred_element_type=F32)
         first_part = coef.astype(BF16).astype(F32)
         target[...] = jnp.concatenate([blank, first_part, coef - first_part], axis=0).astype(BF16)
+    wanted = jnp.broadcast_to(slot_ref[...].astype(F32), (8, GROUP)).T[:, 0:1]
+    unperm[...] = (iota((GROUP, GROUP), 1).astype(F32) == wanted).astype(F32).astype(BF16)
     expand[...] = (iota((16, GROUP), 0) == iota((16, GROUP), 1) // BLOCK).astype(F32).astype(BF16)
     acc[...] = jnp.zeros_like(acc)
 
@@ -200,7 +228,7 @@
     cut4 = inv_cut**4
     cut7 = inv_cut**7
 
-    ahead = 1 - 2 * (v % 2)
+    ahead = (1 - 2 * (v % 2)) * (1 - 2 * count(below))
 
     def wait(slot, width):
         pltpu.make_async_remote_copy(
@@ -290,7 +318,23 @@
             wait(one_slot, LINK)
             wait(two_slot, LINK)
 
-        @pl.when(is_far == 1)
+            @pl.when(late_odd)
+            def _():
+                link(-1, 0).start()
+                link(1, 0).start()
+
+            @pl.when(below)
+            def _():
+                link(-1, 1).start()
+                link(1, 1).start()
+
+            @pl.when(late)
+            def _():
+                wait(1, LINK)
+                for e in (-1, 0, 1):
+                    link(e, -1).start()
+
+        @pl.when((is_far == 1) & jnp.logical_not(late))
         def _():
             wait((ahead + 1) * 3 + 1, LINK)
 
@@ -307,7 +351,7 @@
             wait(one_slot, GROUP)
             wait(two_slot, GROUP)
 
-        @pl.when((is_near == 1) & early)
+        @pl.when(((is_near == 1) & early) | ((is_far == 1) & below))
         def _():
             link(-1, -1).start()
             link(1, -1).start()
@@ -330,7 +374,7 @@
         force += own_z[p] * got[12:13] - pulled
     force = force * KICK_FACTOR
     parts = jnp.concatenate(split3(force), axis=0).astype(BF16)
-    stored = lax.dot_general(parts, perm[...], NT, preferred_element_type=F32)
+    stored = jnp.dot(parts, unperm[...], preferred_element_type=F32)
     out_ref[...] = (stored[0:8] + stored[8:16] + stored[16:24])[0:3]
 
     for e, f in around:
@@ -354,6 +398,7 @@
             pltpu.VMEM((NTYPE, NTYPE), F32),
             pltpu.VMEM((NTYPE, NTYPE), F32),
             pltpu.VMEM((9, 4, LINK), F32),
+            pltpu.VMEM((GROUP, GROUP), BF16),
             pltpu.VMEM((GROUP, GROUP), BF16),
             pltpu.VMEM((8, GROUP), F32),
             pltpu.VMEM((8, BLOCK), I32),

time: 26 us -> 23.5 us (0.904)
  Pallas kernels: 24.5 us -> 22 us
    pallas_call x1, Pallas kernels: 24.5 us -> 22 us  [body(): pl.pallas_call(kernel, out_shape=pltpu.VMEM((3, GROUP), F32), in_specs=[h...]
where the time goes in v4:
time: 23.5 us; the launch traced here: 23.3 us
  Pallas kernels  22 us (94%)
  between operations  0.68 us (3%)
  other arithmetic  0.6 us (3%)
    pallas_call x1, Pallas kernels, body(): pl.pallas_call(kernel, out_shape=pltpu.VMEM((3, GROUP), F32), in_specs=[h...  22 us
    add x1, other arithmetic, body(): return velocities + kick  0.6 us

profile of v4, /device:TPU:1, one launch (start us, length us, event | category | flops | bytes accessed | tf_op | source)
XLA Modules:
  0.0 23.3 jit_solution(4559862720180620880)
XLA Ops:
  0.7 0.0 copy-start
  0.7 22.0 %column_forces.1 = f32[3,512]{1,0:T(4,128)S(1)} custom-call(f32[3,512]{1,0:T(4,128)} %pos_hbm.1, s32[1,512]{1,0:T(1,128)} %bitcast.2, s32[1,512]{1,0:T(1,128)} %bitcast.3, s32[2,72]{1,0:T(2,128)} %pair_hbm.1, s32[1]{0:T(128)S(6)} %copy.9.count_hbm, f32[18,18]{1,0:T(8,128)} %c6_hbm.1, f32[18,18]{1,0:T(8,128)} %c12_hbm.1), custom_call_target="tpu_custom_call" | custom-call | tf_op jit(solution)/shard_map/column_forces/pallas_call | solution.py:387
  22.7 0.0 copy-done
  22.7 0.6 %add.3 = f32[3,512]{1,0:T(4,128)} add(f32[3,512]{1,0:T(4,128)S(1)} %copy-done, f32[3,512]{1,0:T(4,128)S(1)} %column_forces.1) | non-fusion elementwise | flops 1536 | bytes 18432 | tf_op jit(solution)/shard_map/add | solution.py:432
Async XLA Ops:
  0.7 22.1 %copy-start = (f32[3,512]{1,0:T(4,128)S(1)}, f32[3,512]{1,0:T(4,128)}, u32[]{:S(2)}) copy-start(f32[3,512]{1,0:T(4,128)} %param.9) | copy-start | bytes 18436

commit v5 on v4

--- a/solution.py
+++ b/solution.py
@@ -32,14 +32,15 @@
 
 CUT_X = float(np.float32(CUT_SQ + SOFT_CORE))
 FEATURES = 32 + 2 * TYPE_PAD
-LINK = GROUP + 2 * BLOCK
+LINK = GROUP + BLOCK
+TABLE_V = 64
 GROUPS = (
     (0, 0, 256, 0, 256),
     (0, 256, 384, 128, 256),
     (1, 128, 256, 256, 384),
     (1, 256, 512, 256, 512),
 )
-CHUNK = 64
+CHUNK = 128
 NT = (((1,), (1,)), ((), ()))
 
 
@@ -60,51 +61,6 @@
     rec, perm, unperm, stage, pairs, tab, rhs_w, rhs_6, rhs_12, own_z, expand, feat, high, low, acc,
     load_sem, send_sem, recv_sem,
 ):
-    row, col = lax.axis_index("row"), lax.axis_index("col")
-    u = 2 * (col % 8) + col // 8
-    v = 2 * (row % 16) + row // 16
-
-    def device_at(e, f):
-        to_u = (u + e + N_COL) % N_COL
-        to_v = (v + f + N_ROW) % N_ROW
-        return (to_v // 2 + to_v % 2 * 16, to_u // 2 + to_u % 2 * 8)
-
-    around = [(e, f) for f in (-1, 0, 1) for e in (-1, 0, 1) if (e, f) != (0, 0)]
-
-    def slot_of(e, f):
-        return (f + 1) * 3 + e + 1
-
-    early = v % 16 == 0
-    late = v % 16 == 15
-    below = v % 16 == 14
-    lower = v % 16 == 13
-    late_odd = late & (u % 2 == 1)
-    barrier = pltpu.get_barrier_semaphore()
-
-    def greet(e, f):
-        pl.semaphore_signal(barrier, inc=1, device_id=device_at(e, f), device_id_type=MESH)
-
-    greet(0, -1)
-
-    @pl.when(jnp.logical_not(late))
-    def _():
-        greet(-1, -1)
-        greet(1, -1)
-
-    @pl.when(jnp.logical_not(late | below))
-    def _():
-        greet(0, 1)
-
-    @pl.when(jnp.logical_not(late | below | lower))
-    def _():
-        greet(-1, 1)
-        greet(1, 1)
-
-    @pl.when(jnp.logical_not(late & (u % 2 == 0)))
-    def _():
-        greet(-1, 0)
-        greet(1, 0)
-
     loads = [
         pltpu.make_async_copy(source, target, load_sem.at[n])
         for n, (source, target) in enumerate((
@@ -112,9 +68,60 @@
             (count_hbm, count_ref), (c6_hbm, c6_ref), (c12_hbm, c12_ref),
         ))
     ]
-    for load in loads:
+    for load in loads[:5]:
         load.start()
-    for load in loads:
+
+    row, col = lax.axis_index("row"), lax.axis_index("col")
+    u = 2 * (col % 8) + col // 8
+    v = 2 * (row % 16) + row // 16
+
+    def device_at(e, f):
+        to_u = (u + e + N_COL) % N_COL
+        to_v = (v + f + N_ROW) % N_ROW
+        return (to_v // 2 + to_v % 2 * 16, to_u // 2 + to_u % 2 * 8)
+
+    def slot_of(e, f):
+        return (f + 1) * 3 + e + 1
+
+    early = v % 16 == 0
+    late = v % 16 == 15
+    below = v % 16 == 14
+    lower = v % 16 == 13
+    last = v == N_ROW - 1
+    before_last = v == N_ROW - 2
+    even = u % 2 == 0
+    half_heard = late & even & jnp.logical_not(last | (u & 13 == 8))
+    barrier = pltpu.get_barrier_semaphore()
+
+    def greet(e, f):
+        pl.semaphore_signal(barrier, inc=1, device_id=device_at(e, f), device_id_type=MESH)
+
+    greet(0, -1)
+
+    @pl.when(jnp.logical_not(late))
+    def _():
+        greet(-1, -1)
+        greet(1, -1)
+
+    @pl.when(jnp.logical_not(late | before_last))
+    def _():
+        greet(0, 1)
+
+    for e in (-1, 1):
+        to_half_heard = below & jnp.logical_not(even | ((u + e) & 13 == 8))
+
+        @pl.when(jnp.logical_not(late | before_last | lower | to_half_heard))
+        def _():
+            greet(e, 1)
+
+    @pl.when(jnp.logical_not(late))
+    def _():
+        greet(-1, 0)
+        greet(1, 0)
+
+    for load in loads[5:]:
+        load.start()
+    for load in loads[:5]:
         load.wait()
 
     perm[...] = (iota((GROUP, GROUP), 0) == slot_ref[...]).astype(F32).astype(BF16)
@@ -151,11 +158,11 @@
         right = jnp.where(full == at, 1.0, 0.0).astype(BF16)
         return lax.dot_general(left, right, NT, preferred_element_type=F32)
 
-    rec[4, :, GROUP : GROUP + BLOCK] = table(ka, du * 16 + dv * 4 + kb)[0:4]
-    rec[4, :, GROUP + BLOCK : LINK] = table(kb, dv * 16 + du * 4 + ka)[0:4]
-
-    def link(e, f):
-        width = GROUP if e and f else LINK
+    tables = table(ka, du * 16 + dv * 4 + kb) + table(kb, TABLE_V + dv * 16 + du * 4 + ka)
+    rec[4, :, GROUP:LINK] = tables[0:4]
+
+    def link(e, f, width=None):
+        width = width or (GROUP if e and f else LINK)
         return pltpu.make_async_remote_copy(
             src_ref=rec.at[4, :, pl.ds(0, width)],
             dst_ref=rec.at[slot_of(-e, -f), :, pl.ds(0, width)],
@@ -165,27 +172,42 @@
             device_id_type=MESH,
         )
 
+    def forward(e, f, width):
+        return pltpu.make_async_remote_copy(
+            src_ref=rec.at[slot_of(e, f), :, pl.ds(0, width)],
+            dst_ref=rec.at[slot_of(e, f + 1), :, pl.ds(0, width)],
+            send_sem=send_sem.at[slot_of(e, -1) if f == 0 else 9 + (e + 1) // 2],
+            recv_sem=recv_sem.at[slot_of(e, f + 1)],
+            device_id=device_at(0, -1),
+            device_id_type=MESH,
+        )
+
     count = lambda flag: flag.astype(I32)
-    expected = 8 - 3 * count(early) - 3 * count(late) - 2 * count(late_odd) - 4 * count(below)
+    expected = 8 - 3 * count(early) - 2 * count(late) - 3 * count(last) - 4 * count(below) - 2 * count(half_heard)
     pl.semaphore_wait(barrier, expected)
 
+    @pl.when(late)
+    def _():
+        link(-1, 1, LINK).start()
+        link(1, 1, LINK).start()
+
     link(0, 1).start()
 
-    @pl.when(jnp.logical_not(below))
+    @pl.when(jnp.logical_not(late | below))
     def _():
         link(-1, 1).start()
         link(1, 1).start()
 
-    @pl.when(jnp.logical_not(early | late))
+    @pl.when(jnp.logical_not(early | last))
     def _():
         link(0, -1).start()
 
-    @pl.when(jnp.logical_not(early | late | below))
+    @pl.when(jnp.logical_not(early | last | half_heard | below))
     def _():
         link(-1, -1).start()
         link(1, -1).start()
 
-    @pl.when(jnp.logical_not(late_odd))
+    @pl.when(jnp.logical_not(late))
     def _():
         link(-1, 0).start()
         link(1, 0).start()
@@ -211,6 +233,8 @@
         ]
         rhs_w[p] = jnp.concatenate(sides, axis=0).astype(BF16)
 
+    for load in loads[5:]:
+        load.wait()
     kinds = (iota((TYPE_PAD, GROUP), 0).astype(F32) == own[3:4]).astype(F32)
     blank = jnp.zeros((32, GROUP), F32)
     for source, target, factor in ((c6_ref, rhs_6, 6.0), (c12_ref, rhs_12, 12.0)):
@@ -228,7 +252,7 @@
     cut4 = inv_cut**4
     cut7 = inv_cut**7
 
-    ahead = (1 - 2 * (v % 2)) * (1 - 2 * count(below))
+    ahead = (1 - 2 * (v % 2)) * (1 - 2 * count(before_last))
 
     def wait(slot, width):
         pltpu.make_async_remote_copy(
@@ -240,10 +264,10 @@
 
     def features(slot, at, scale):
         e, f = slot % 3 - 1, slot // 3 - 1
-        tab_u = rec[3 + e + 1, :, GROUP : GROUP + BLOCK]
-        tab_v = rec[(f + 1) * 3 + 1, :, GROUP + BLOCK : LINK]
+        tab_u = rec[3 + e + 1, :, GROUP:LINK]
+        tab_v = rec[(f + 1) * 3 + 1, :, GROUP:LINK]
         shift_u = BLOCK - ((1 - e) * 16 + (1 + f) * 4)
-        shift_v = BLOCK - ((1 - f) * 16 + (1 + e) * 4)
+        shift_v = BLOCK - (TABLE_V + (1 - f) * 16 + (1 + e) * 4)
         tab_u = pltpu.roll(jnp.concatenate([tab_u, tab_u], axis=0), shift_u, 1)
         tab_v = pltpu.roll(jnp.concatenate([tab_v, tab_v], axis=0), shift_v, 1)
         seen = (tab_u + tab_v)[:, 0:16]
@@ -268,9 +292,9 @@
         rows = jnp.concatenate(
             [high_mid, jnp.where(upper, h, l), high_mid, jnp.ones((8, GROUP), F32), onehot, onehot],
             axis=0,
-        )
+        ).astype(BF16)
         for k in range(BPD):
-            feat[at, k * BLOCK : (k + 1) * BLOCK, :] = rows[:, k * BLOCK : (k + 1) * BLOCK].T.astype(BF16)
+            feat[at, k * BLOCK : (k + 1) * BLOCK, :] = rows[:, k * BLOCK : (k + 1) * BLOCK].T
         back = jnp.concatenate([high_mid, jnp.where(upper, l, 1.0)], axis=0)
         return back, weight
 
@@ -305,36 +329,37 @@
 
     def two_columns(t, carry):
         is_u = (t == 1).astype(I32)
-        is_far = (t == 2).astype(I32)
-        is_side = (t == 3).astype(I32)
+        side_at = 3 - count(v == 0)
+        is_far = (t == 5 - side_at).astype(I32)
+        is_side = (t == side_at).astype(I32)
         is_near = (t == 4).astype(I32)
         e = is_u + is_far + is_near
         f = is_far * ahead - is_near * ahead
         one_slot = (f + is_side * ahead + 1) * 3 + 1 - e
         two_slot = (f - is_side * ahead + 1) * 3 + 1 + e
 
+        @pl.when((is_u == 1) & (last | half_heard))
+        def _():
+            wait(1, LINK)
+            link(-1, -1).start()
+            link(1, -1).start()
+
+            @pl.when(last)
+            def _():
+                link(0, -1).start()
+
         @pl.when(is_u == 1)
         def _():
             wait(one_slot, LINK)
             wait(two_slot, LINK)
 
-            @pl.when(late_odd)
-            def _():
-                link(-1, 0).start()
-                link(1, 0).start()
-
             @pl.when(below)
             def _():
-                link(-1, 1).start()
-                link(1, 1).start()
-
-            @pl.when(late)
-            def _():
-                wait(1, LINK)
-                for e in (-1, 0, 1):
-                    link(e, -1).start()
-
-        @pl.when((is_far == 1) & jnp.logical_not(late))
+                for f in (-1, 1):
+                    link(-1, f).start()
+                    link(1, f).start()
+
+        @pl.when((t == 2) & jnp.logical_not(last | half_heard))
         def _():
             wait((ahead + 1) * 3 + 1, LINK)
 
@@ -345,23 +370,28 @@
             @pl.when(early)
             def _():
                 link(0, -1).start()
-
-        @pl.when(is_far + is_near == 1)
+                forward(-1, 0, GROUP).start()
+                forward(1, 0, GROUP).start()
+
+        from_late = (is_near == 1) & early
+
+        @pl.when((is_far + is_near == 1) & jnp.logical_not(from_late))
         def _():
             wait(one_slot, GROUP)
             wait(two_slot, GROUP)
 
-        @pl.when(((is_near == 1) & early) | ((is_far == 1) & below))
-        def _():
-            link(-1, -1).start()
-            link(1, -1).start()
+        @pl.when(from_late)
+        def _():
+            for side in (-1, 1):
+                wait(slot_of(side, -1), LINK)
+                forward(side, -1, LINK).start()
 
         scale = jnp.minimum(t, 1).astype(F32)
         first_side = features(one_slot, 0, 1.0)
         second_side = features(two_slot, 1, scale)
         scalars(0)
+        sums(0, *first_side)
         scalars(1)
-        sums(0, *first_side)
         sums(1, *second_side)
         return carry
 
@@ -377,8 +407,25 @@
     stored = jnp.dot(parts, unperm[...], preferred_element_type=F32)
     out_ref[...] = (stored[0:8] + stored[8:16] + stored[16:24])[0:3]
 
-    for e, f in around:
-        link(e, f).wait_send()
+    for e in (-1, 0, 1):
+        link(e, -1).wait_send()
+    link(0, 1).wait_send()
+
+    @pl.when(late)
+    def _():
+        link(-1, 1, LINK).wait_send()
+        link(1, 1, LINK).wait_send()
+
+    @pl.when(jnp.logical_not(late))
+    def _():
+        for e in (-1, 1):
+            link(e, 1).wait_send()
+            link(e, 0).wait_send()
+
+    @pl.when(early)
+    def _():
+        forward(-1, -1, LINK).wait_send()
+        forward(1, -1, LINK).wait_send()
 
 
 def body(positions, velocities, bead_types, slot_bead, tile_pairs, tile_count, c6_table, c12_table):
@@ -413,7 +460,7 @@
             pltpu.VMEM((2, GROUP, GROUP), BF16),
             pltpu.VMEM((2, 16, GROUP), F32),
             pltpu.SemaphoreType.DMA((7,)),
-            pltpu.SemaphoreType.DMA((9,)),
+            pltpu.SemaphoreType.DMA((11,)),
             pltpu.SemaphoreType.DMA((9,)),
         ],
         compiler_params=pltpu.CompilerParams(

time: 23.5 us -> 23 us (0.979)
  Pallas kernels: 22 us -> 21.5 us
    pallas_call x1, Pallas kernels: 22 us -> 21.5 us  [body(): pl.pallas_call(kernel, out_shape=pltpu.VMEM((3, GROUP), F32), in_specs=[h...]
where the time goes in v5:
time: 23 us; the launch traced here: 22.8 us
  Pallas kernels  21.5 us (93%)
  between operations  0.68 us (3%)
  other arithmetic  0.6 us (3%)
    pallas_call x1, Pallas kernels, body(): pl.pallas_call(kernel, out_shape=pltpu.VMEM((3, GROUP), F32), in_specs=[h...  21.5 us
    add x1, other arithmetic, body(): return velocities + kick  0.6 us

profile of v5, /device:TPU:1, one launch (start us, length us, event | category | flops | bytes accessed | tf_op | source)
XLA Modules:
  0.0 22.8 jit_solution(4523829751727905934)
XLA Ops:
  0.7 0.0 copy-start
  0.7 21.5 %column_forces.1 = f32[3,512]{1,0:T(4,128)S(1)} custom-call(f32[3,512]{1,0:T(4,128)} %pos_hbm.1, s32[1,512]{1,0:T(1,128)} %bitcast.2, s32[1,512]{1,0:T(1,128)} %bitcast.3, s32[2,72]{1,0:T(2,128)} %pair_hbm.1, s32[1]{0:T(128)S(6)} %copy.9.count_hbm, f32[18,18]{1,0:T(8,128)} %c6_hbm.1, f32[18,18]{1,0:T(8,128)} %c12_hbm.1), custom_call_target="tpu_custom_call" | custom-call | tf_op jit(solution)/shard_map/column_forces/pallas_call | solution.py:434
  22.2 0.0 copy-done
  22.2 0.6 %add.3 = f32[3,512]{1,0:T(4,128)} add(f32[3,512]{1,0:T(4,128)S(1)} %copy-done, f32[3,512]{1,0:T(4,128)S(1)} %column_forces.1) | non-fusion elementwise | flops 1536 | bytes 18432 | tf_op jit(solution)/shard_map/add | solution.py:479
Async XLA Ops:
  0.7 21.5 %copy-start = (f32[3,512]{1,0:T(4,128)S(1)}, f32[3,512]{1,0:T(4,128)}, u32[]{:S(2)}) copy-start(f32[3,512]{1,0:T(4,128)} %param.9) | copy-start | bytes 18436

commit v6 on v5

--- a/solution.py
+++ b/solution.py
@@ -121,10 +121,10 @@
 
     for load in loads[5:]:
         load.start()
-    for load in loads[:5]:
+    loads[0].wait()
+    perm[...] = (iota((GROUP, GROUP), 0) == slot_ref[...]).astype(F32).astype(BF16)
+    for load in loads[1:5]:
         load.wait()
-
-    perm[...] = (iota((GROUP, GROUP), 0) == slot_ref[...]).astype(F32).astype(BF16)
     stage[...] = jnp.zeros_like(stage)
     stage[0:3, :] = pos_ref[...]
     stage[3:4, :] = typ_ref[...].astype(F32)
@@ -153,13 +153,13 @@
     eight = iota((8, BLOCK), 0)
     full = iota((BLOCK, BLOCK), 0)
 
-    def table(layer_at, at):
-        left = jnp.where((eight == layer_at) & live, 1.0, 0.0).astype(BF16)
-        right = jnp.where(full == at, 1.0, 0.0).astype(BF16)
-        return lax.dot_general(left, right, NT, preferred_element_type=F32)
-
-    tables = table(ka, du * 16 + dv * 4 + kb) + table(kb, TABLE_V + dv * 16 + du * 4 + ka)
-    rec[4, :, GROUP:LINK] = tables[0:4]
+    left = jnp.concatenate([eight == ka, eight == kb], axis=1)
+    left = jnp.where(left & jnp.concatenate([live, live], axis=1), 1.0, 0.0).astype(BF16)
+    at_u = du * 16 + dv * 4 + kb
+    at_v = TABLE_V + dv * 16 + du * 4 + ka
+    right = jnp.concatenate([full == at_u, full == at_v], axis=1)
+    right = jnp.where(right, 1.0, 0.0).astype(BF16)
+    rec[4, :, GROUP:LINK] = lax.dot_general(left, right, NT, preferred_element_type=F32)[0:4]
 
     def link(e, f, width=None):
         width = width or (GROUP if e and f else LINK)
@@ -403,9 +403,10 @@
         pulled = got[0:8] + pltpu.roll(got[0:8], 4, 0) + got[8:16]
         force += own_z[p] * got[12:13] - pulled
     force = force * KICK_FACTOR
-    parts = jnp.concatenate(split3(force), axis=0).astype(BF16)
+    coarse = force.astype(BF16).astype(F32)
+    parts = jnp.concatenate([coarse, force - coarse], axis=0).astype(BF16)
     stored = jnp.dot(parts, unperm[...], preferred_element_type=F32)
-    out_ref[...] = (stored[0:8] + stored[8:16] + stored[16:24])[0:3]
+    out_ref[...] = (stored[0:8] + stored[8:16])[0:3]
 
     for e in (-1, 0, 1):
         link(e, -1).wait_send()

time: 23 us -> 23.1 us (level)
  no operation moved by 1% of the time
where the time goes in v6:
time: 23.1 us; the launch traced here: 22.9 us
  Pallas kernels  21.6 us (94%)
  between operations  0.68 us (3%)
  other arithmetic  0.6 us (3%)
    pallas_call x1, Pallas kernels, body(): pl.pallas_call(kernel, out_shape=pltpu.VMEM((3, GROUP), F32), in_specs=[h...  21.6 us
    add x1, other arithmetic, body(): return velocities + kick  0.6 us

profile of v6, /device:TPU:1, one launch (start us, length us, event | category | flops | bytes accessed | tf_op | source)
XLA Modules:
  0.0 22.9 jit_solution(15646953758992148511)
XLA Ops:
  0.7 0.0 copy-start
  0.7 21.6 %column_forces.1 = f32[3,512]{1,0:T(4,128)S(1)} custom-call(f32[3,512]{1,0:T(4,128)} %pos_hbm.1, s32[1,512]{1,0:T(1,128)} %bitcast.2, s32[1,512]{1,0:T(1,128)} %bitcast.3, s32[2,72]{1,0:T(2,128)} %pair_hbm.1, s32[1]{0:T(128)S(6)} %copy.9.count_hbm, f32[18,18]{1,0:T(8,128)} %c6_hbm.1, f32[18,18]{1,0:T(8,128)} %c12_hbm.1), custom_call_target="tpu_custom_call" | custom-call | tf_op jit(solution)/shard_map/column_forces/pallas_call | solution.py:435
  22.3 0.0 copy-done
  22.3 0.6 %add.3 = f32[3,512]{1,0:T(4,128)} add(f32[3,512]{1,0:T(4,128)S(1)} %copy-done, f32[3,512]{1,0:T(4,128)S(1)} %column_forces.1) | non-fusion elementwise | flops 1536 | bytes 18432 | tf_op jit(solution)/shard_map/add | solution.py:480
Async XLA Ops:
  0.7 21.6 %copy-start = (f32[3,512]{1,0:T(4,128)S(1)}, f32[3,512]{1,0:T(4,128)}, u32[]{:S(2)}) copy-start(f32[3,512]{1,0:T(4,128)} %param.9) | copy-start | bytes 18436

commit v7 on v6

--- a/solution.py
+++ b/solution.py
@@ -188,8 +188,8 @@
 
     @pl.when(late)
     def _():
+        link(1, 1, LINK).start()
         link(-1, 1, LINK).start()
-        link(1, 1, LINK).start()
 
     link(0, 1).start()
 
@@ -329,7 +329,7 @@
 
     def two_columns(t, carry):
         is_u = (t == 1).astype(I32)
-        side_at = 3 - count(v == 0)
+        side_at = 3 - count((v == 0) & (u == 2))
         is_far = (t == 5 - side_at).astype(I32)
         is_side = (t == side_at).astype(I32)
         is_near = (t == 4).astype(I32)

time: 23.1 us -> 22.8 us (0.987)
  Pallas kernels: 21.6 us -> 21.3 us
    pallas_call x1, Pallas kernels: 21.6 us -> 21.3 us  [body(): pl.pallas_call(kernel, out_shape=pltpu.VMEM((3, GROUP), F32), in_specs=[h...]
where the time goes in v7:
time: 22.8 us; the launch traced here: 22.6 us
  Pallas kernels  21.3 us (93%)
  between operations  0.68 us (3%)
  other arithmetic  0.6 us (3%)
    pallas_call x1, Pallas kernels, body(): pl.pallas_call(kernel, out_shape=pltpu.VMEM((3, GROUP), F32), in_specs=[h...  21.3 us
    add x1, other arithmetic, body(): return velocities + kick  0.6 us

profile of v7, /device:TPU:1, one launch (start us, length us, event | category | flops | bytes accessed | tf_op | source)
XLA Modules:
  0.0 22.6 jit_solution(11102793990092919281)
XLA Ops:
  0.7 0.0 copy-start
  0.7 21.3 %column_forces.1 = f32[3,512]{1,0:T(4,128)S(1)} custom-call(f32[3,512]{1,0:T(4,128)} %pos_hbm.1, s32[1,512]{1,0:T(1,128)} %bitcast.2, s32[1,512]{1,0:T(1,128)} %bitcast.3, s32[2,72]{1,0:T(2,128)} %pair_hbm.1, s32[1]{0:T(128)S(6)} %copy.9.count_hbm, f32[18,18]{1,0:T(8,128)} %c6_hbm.1, f32[18,18]{1,0:T(8,128)} %c12_hbm.1), custom_call_target="tpu_custom_call" | custom-call | tf_op jit(solution)/shard_map/column_forces/pallas_call | solution.py:435
  22.0 0.0 copy-done
  22.0 0.6 %add.3 = f32[3,512]{1,0:T(4,128)} add(f32[3,512]{1,0:T(4,128)S(1)} %copy-done, f32[3,512]{1,0:T(4,128)S(1)} %column_forces.1) | non-fusion elementwise | flops 1536 | bytes 18432 | tf_op jit(solution)/shard_map/add | solution.py:480
Async XLA Ops:
  0.7 21.3 %copy-start = (f32[3,512]{1,0:T(4,128)S(1)}, f32[3,512]{1,0:T(4,128)}, u32[]{:S(2)}) copy-start(f32[3,512]{1,0:T(4,128)} %param.9) | copy-start | bytes 18436

commit v8 on v7

--- a/solution.py
+++ b/solution.py
@@ -382,7 +382,7 @@
 
         @pl.when(from_late)
         def _():
-            for side in (-1, 1):
+            for side in (1, -1):
                 wait(slot_of(side, -1), LINK)
                 forward(side, -1, LINK).start()
 

time: 22.8 us -> 22.8 us (level)
  no operation moved by 1% of the time
where the time goes in v8:
time: 22.8 us; the launch traced here: 22.6 us
  Pallas kernels  21.3 us (93%)
  between operations  0.68 us (3%)
  other arithmetic  0.6 us (3%)
    pallas_call x1, Pallas kernels, body(): pl.pallas_call(kernel, out_shape=pltpu.VMEM((3, GROUP), F32), in_specs=[h...  21.3 us
    add x1, other arithmetic, body(): return velocities + kick  0.6 us

profile of v8, /device:TPU:1, one launch (start us, length us, event | category | flops | bytes accessed | tf_op | source)
XLA Modules:
  0.0 22.6 jit_solution(8047063674701396025)
XLA Ops:
  0.7 0.0 copy-start
  0.7 21.3 %column_forces.1 = f32[3,512]{1,0:T(4,128)S(1)} custom-call(f32[3,512]{1,0:T(4,128)} %pos_hbm.1, s32[1,512]{1,0:T(1,128)} %bitcast.2, s32[1,512]{1,0:T(1,128)} %bitcast.3, s32[2,72]{1,0:T(2,128)} %pair_hbm.1, s32[1]{0:T(128)S(6)} %copy.9.count_hbm, f32[18,18]{1,0:T(8,128)} %c6_hbm.1, f32[18,18]{1,0:T(8,128)} %c12_hbm.1), custom_call_target="tpu_custom_call" | custom-call | tf_op jit(solution)/shard_map/column_forces/pallas_call | solution.py:435
  22.0 0.0 copy-done
  22.0 0.6 %add.3 = f32[3,512]{1,0:T(4,128)} add(f32[3,512]{1,0:T(4,128)S(1)} %copy-done, f32[3,512]{1,0:T(4,128)S(1)} %column_forces.1) | non-fusion elementwise | flops 1536 | bytes 18432 | tf_op jit(solution)/shard_map/add | solution.py:480
Async XLA Ops:
  0.7 21.3 %copy-start = (f32[3,512]{1,0:T(4,128)S(1)}, f32[3,512]{1,0:T(4,128)}, u32[]{:S(2)}) copy-start(f32[3,512]{1,0:T(4,128)} %param.9) | copy-start | bytes 18436
